TPU v7x, 256 devices: a whole 4x4x8 slice. The times are simulated.
256 devices in a mesh: view: 16 (over x_lo, z), seq: 16 (over y, x_hi, core).
Axes of the slice: x: 4 (x_hi: 2, x_lo: 2; x = x_hi * 2 + x_lo), y: 4, z: 8, core: 2. Of those that a mesh axis runs over, the one named last changes fastest.
Arguments:
- tokens: bfloat16 [16, 6144, 1024], P('view', 'seq'), may hold values from -6 to 6
- w_cross_qkv: bfloat16 [1024, 3072], replicated, may hold values from -8 to 8
- w_cross_out: bfloat16 [1024, 1024], replicated, may hold values from -3 to 3
- w_temporal_qkv: bfloat16 [1024, 3072], P('view'), may hold values from -8 to 8
- w_temporal_out: bfloat16 [1024, 1024], P('view'), may hold values from -0.359375 to 0.359375
Outputs:
- cross_update: bfloat16 [16, 6144, 1024], P('view', 'seq')
- temporal_update: bfloat16 [16, 6144, 1024], P('view', 'seq')
All inputs are finite; a program needn't handle non-finite values.
Results may differ from a plain program's by a relative error of at most 0.02.
Values may be sent and summed in bfloat16 or wider, within the bound.
No kernel may reach another device: no remote copies, remote signals or barrier semaphores. Data moves between devices by JAX's collectives and lax.ppermute only.
A program may use at most 128 MiB of HBM per device.

v0:
```python
import functools

import jax
import jax.numpy as jnp
from jax import lax
from jax.experimental import pallas as pl
from jax.experimental.pallas import tpu as pltpu
from jax.sharding import Mesh
from jax.sharding import PartitionSpec as P

HEADS = 16
HD = 64
PAIR = 2 * HD
QUAD = 4 * HD
LOG2E = 1.4426950408889634
CROSS_LIMIT = 24 * 1024 * 1024
UNROLL = 2
F32 = jnp.float32
BF16 = jnp.bfloat16


def dot(a, b):
    return jnp.dot(a, b, preferred_element_type=F32)


def layer_norm(rows):
    centred = rows - jnp.mean(rows, axis=-1, keepdims=True)
    variance = jnp.mean(centred * centred, axis=-1, keepdims=True)
    return (centred * lax.rsqrt(variance + 1e-06)).astype(BF16)


def lanes_of(width, index, rows=1):
    lane = lax.broadcasted_iota(jnp.int32, (rows, width), 1)
    return jnp.where(lane // HD == index, 1.0, 0.0).astype(BF16)


def project_blocks(x_refs, w_refs, norm_s, q_ref, kt_s, v_s):
    pairs, _, keys = kt_s.shape
    start = 0
    for x_ref in x_refs:
        norm_s[start : start + x_ref.shape[0], :] = layer_norm(x_ref[...].astype(F32))
        start += x_ref.shape[0]

    def project(which, quad):
        return dot(norm_s[...], w_refs[which][:, quad * QUAD : (quad + 1) * QUAD])

    for quad in range(pairs // 2):
        if q_ref is not None:
            made = (project(2, quad) * (HD**-0.5 * LOG2E)).astype(BF16)
            for part in range(2):
                q_ref[2 * quad + part] = made[:, part * PAIR : (part + 1) * PAIR]
        made = project(0, quad).astype(BF16)
        for part in range(2):
            kt_s[2 * quad + part] = made[:, part * PAIR : (part + 1) * PAIR].T
        made = project(1, quad).astype(BF16)
        for part in range(2):
            v_s[2 * quad + part, :, :PAIR] = made[:, part * PAIR : (part + 1) * PAIR]
            v_s[2 * quad + part, :, PAIR:] = jnp.ones((keys, PAIR), BF16)


def attend_pairs(q_ref, kt_s, v_s, state, outs, row_block, part=None):
    pairs, count = q_ref.shape[:2]
    begin, end = (0, count) if part is None else (part * count // 2, (part + 1) * count // 2)
    low = lax.broadcasted_iota(jnp.int32, (row_block, PAIR), 1) < HD

    def attend(pair, carry):
        transposed, values = kt_s[pair], v_s[pair]
        for start in range(begin, end, row_block):
            rows = slice(start, start + row_block)
            queries = q_ref[pair, rows, :]
            peaks, sums = [], []
            for head in range(2):
                scores = dot(queries * lanes_of(PAIR, head), transposed)
                peak = jnp.max(scores, axis=-1, keepdims=True)
                weights = jnp.exp2(scores - peak).astype(BF16)
                peaks.append(peak)
                sums.append(dot(weights, values))
            peak = jnp.where(low, peaks[0], peaks[1])
            result = jnp.where(low, sums[0][:, :PAIR], sums[1][:, :PAIR])
            total = jnp.where(low, sums[0][:, PAIR:], sums[1][:, PAIR:])
            if state is not None:
                o_in, m_in, l_in = state
                highest = jnp.maximum(peak, m_in[pair, rows, :])
                old, new = jnp.exp2(m_in[pair, rows, :] - highest), jnp.exp2(peak - highest)
                result = new * result + old * o_in[pair, rows, :]
                total = new * total + old * l_in[pair, rows, :]
                peak = highest
            if part is not None:
                offset = start - begin
                outs[0][pair, offset : offset + row_block, :] = (result / total).astype(BF16)
            else:
                for out, value in zip(outs, (result, peak, total)):
                    out[pair, rows, :] = value
        return carry

    lax.fori_loop(0, pairs, attend, 0, unroll=UNROLL)


def project_kernel(x0_ref, x1_ref, wk_ref, wv_ref, wq_ref, q_ref, kt_ref, v_ref, norm_s):
    project_blocks((x0_ref, x1_ref), (wk_ref, wv_ref, wq_ref), norm_s, q_ref, kt_ref, v_ref)


def attend_kernel(row_block, q_ref, kt_ref, v_ref, *outs):
    attend_pairs(q_ref, kt_ref, v_ref, None, outs, row_block)


def project_more_kernel(blocks, *refs):
    x_refs, w_refs, (kt_ref, v_ref, norm_s) = refs[:blocks], refs[blocks:-3], refs[-3:]
    project_blocks(x_refs, w_refs, norm_s, None, kt_ref, v_ref)


def finish_kernel(row_block, part, q_ref, kt_ref, v_ref, o_ref, m_ref, l_ref, out_ref):
    attend_pairs(q_ref, kt_ref, v_ref, (o_ref, m_ref, l_ref), (out_ref,), row_block, part)


VMEM_SPEC = pl.BlockSpec(memory_space=pltpu.VMEM)
SMEM_SPEC = pl.BlockSpec(memory_space=pltpu.SMEM)


def local_kernel(kernel, name, operands, out_shape, scratch_shapes=(), scalars=0):
    return pl.pallas_call(
        kernel,
        in_specs=[SMEM_SPEC] * scalars + [VMEM_SPEC] * (len(operands) - scalars),
        out_specs=[VMEM_SPEC] * len(out_shape),
        scratch_shapes=list(scratch_shapes),
        out_shape=out_shape,
        compiler_params=pltpu.CompilerParams(vmem_limit_bytes=CROSS_LIMIT),
        cost_estimate=pl.CostEstimate(flops=10**6, bytes_accessed=10**5, transcendentals=0),
        name=name,
    )(*operands)


def cross_project(xs, weights):
    features, columns = weights[0].shape
    keys = sum(x.shape[0] for x in xs)
    pairs = columns // PAIR
    shapes = ((pairs, keys, PAIR), (pairs, PAIR, keys), (pairs, keys, 2 * PAIR))
    first = len(weights) == 3
    out_shape = [jax.ShapeDtypeStruct(shape, BF16) for shape in shapes[0 if first else 1 :]]
    scratch = [pltpu.VMEM((keys, features), BF16)]
    kernel = project_kernel if first else functools.partial(project_more_kernel, len(xs))
    name = "cross_project" if first else "cross_project_more"
    return local_kernel(kernel, name, (*xs, *weights), out_shape, scratch)


def cross_attend(queries, projected, state=None, part=None, row_block=384):
    pairs, count, width = queries.shape
    operands = (queries, *projected)
    if state is None:
        kept = [jax.ShapeDtypeStruct(queries.shape, F32)] * 3
        kernel = functools.partial(attend_kernel, row_block)
        return local_kernel(kernel, "cross_attend", operands, kept)
    out_shape = [jax.ShapeDtypeStruct((pairs, count // 2, width), BF16)]
    kernel = functools.partial(finish_kernel, row_block, part)
    return local_kernel(kernel, "cross_finish", (*operands, *state), out_shape)[0]


def cross_out_kernel(core_ref, mine_ref, other_ref, x_ref, w_ref, cross_ref, norm_ref):
    pairs = mine_ref.shape[0]
    half = pairs * PAIR
    made = None
    for ref, core in ((mine_ref, core_ref[0]), (other_ref, 1 - core_ref[0])):
        rows = jnp.concatenate([ref[pair] for pair in range(pairs)], axis=-1)
        part = dot(rows, w_ref[pl.ds(pl.multiple_of(core * half, half), half), :])
        made = part if made is None else made + part
    cross_ref[...] = made.astype(BF16)
    residual = x_ref[...].astype(F32) + cross_ref[...].astype(F32)
    norm_ref[...] = layer_norm(residual)


def cross_out(core, mine, other, tokens, w_cross_out):
    out_shape = [jax.ShapeDtypeStruct(tokens.shape, BF16)] * 2
    operands = (core, mine, other, tokens, w_cross_out)
    return local_kernel(cross_out_kernel, "cross_out", operands, out_shape, scalars=1)


GROUP = 16
BLOCKS = 16


def halves(ref, own_half):
    half = ref.shape[1] // 2
    return [
        ref[:, pl.ds(pl.multiple_of(which * half, half), half)]
        for which in (own_half, 1 - own_half)
    ]


def times(ref, w_ref, columns, own_half):
    block = w_ref.shape[0] // BLOCKS
    made = None
    for side, rows in enumerate(halves(ref, own_half)):
        starts = range(side * block, w_ref.shape[0], 2 * block)
        part = jnp.concatenate([w_ref[start : start + block, columns] for start in starts], axis=0)
        made = dot(rows, part) if made is None else made + dot(rows, part)
    return made


def grouped(shape):
    frames, positions, _ = shape
    for group in range(positions // GROUP):
        for frame in range(frames):
            start = (group * frames + frame) * GROUP
            yield slice(start, start + GROUP), frame, slice(group * GROUP, (group + 1) * GROUP)


def temporal_heads(x_ref, w_ref, own_half, x_s, store):
    frames, positions, features = x_ref.shape
    size = frames * GROUP
    half = features // 2
    heads = QUAD // HD
    for rows, frame, place in grouped(x_ref.shape):
        x_s[rows, :] = x_ref[frame, place, :]
    row = lax.broadcasted_iota(jnp.int32, (heads * size, size), 0)
    column = lax.broadcasted_iota(jnp.int32, (heads * size, size), 1)
    same = row % GROUP == column % GROUP
    head_of = lax.broadcasted_iota(jnp.int32, (size, QUAD), 1) // HD
    for quad in range(half // QUAD):

        def project(which):
            start = which * half + quad * QUAD
            return times(x_s, w_ref, slice(start, start + QUAD), own_half)

        queries = (project(0) * (HD**-0.5 * LOG2E)).astype(BF16)
        keys = project(1).astype(BF16)
        values = project(2).astype(BF16)
        for group in range(positions // GROUP):
            part = slice(group * size, (group + 1) * size)
            stacked = jnp.concatenate(
                [queries[part] * lanes_of(QUAD, head) for head in range(heads)], axis=0
            )
            scores = jnp.where(same, dot(stacked, keys[part].T), -jnp.inf)
            weights = jnp.exp2(scores - jnp.max(scores, axis=-1, keepdims=True))
            total = jnp.sum(weights, axis=-1, keepdims=True)
            result = dot(weights.astype(BF16), values[part]) / total
            attended = result[:size]
            for head in range(1, heads):
                attended = jnp.where(
                    head_of == head, result[head * size : (head + 1) * size], attended
                )
            store(part, quad * QUAD, attended.astype(BF16))


def temporal_mine_kernel(place_ref, x_ref, w_ref, att_ref, x_s):
    def store(rows, start, value):
        att_ref[rows, start : start + QUAD] = value

    temporal_heads(x_ref, w_ref, place_ref[1], x_s, store)


def temporal_other_kernel(place_ref, x_ref, wm_ref, wo_ref, att_ref, out_ref, x_s, att_s):
    features = x_ref.shape[2]
    half = features // 2
    core, own_half = place_ref[0], place_ref[1]
    mine, other = pl.multiple_of(core * half, half), pl.multiple_of((1 - core) * half, half)
    att_s[:, pl.ds(mine, half)] = att_ref[...]

    def store(rows, start, value):
        att_s[rows, pl.ds(pl.multiple_of(other + start, QUAD), QUAD)] = value

    temporal_heads(x_ref, wo_ref, own_half, x_s, store)
    for start, w_ref in ((mine, wm_ref), (other, wo_ref)):
        made = times(att_s, w_ref, slice(3 * half, 4 * half), own_half).astype(BF16)
        for rows, frame, place in grouped(x_ref.shape):
            out_ref[frame, place, pl.ds(start, half)] = made[rows]


def assemble_kernel(place_ref, *refs):
    blocks, out_ref = refs[:-1], refs[-1]
    size = blocks[0].shape[0]
    count = out_ref.shape[0] // size
    own = place_ref[2]

    def rows(step, start, length):
        index = lax.rem(own + step + count, count)
        return pl.ds(pl.multiple_of(index * size + start, length), length)

    for ref, step in zip(blocks, (0, -1, 1, -2, 2, -3, 3, 4)):
        out_ref[rows(step, 0, size), :] = ref[...]


def assemble(place, blocks):
    size, columns = blocks[0].shape
    out_shape = [jax.ShapeDtypeStruct((8 * size, columns), BF16)]
    return local_kernel(assemble_kernel, "assemble", (place, *blocks), out_shape, (), 1)[0]


def temporal_mine(place, rows, weights):
    frames, positions, features = rows.shape
    count = frames * positions
    out_shape = [jax.ShapeDtypeStruct((count, features // 2), BF16)]
    scratch = [pltpu.VMEM((count, features), BF16)]
    operands = (place, rows, weights)
    return local_kernel(temporal_mine_kernel, "temporal_mine", operands, out_shape, scratch, 1)[0]


def temporal_other(place, rows, mine, other, attended):
    frames, positions, features = rows.shape
    out_shape = [jax.ShapeDtypeStruct(rows.shape, BF16)]
    scratch = [pltpu.VMEM((frames * positions, features), BF16)] * 2
    operands = (place, rows, mine, other, attended)
    return local_kernel(temporal_other_kernel, "temporal_other", operands, out_shape, scratch, 1)[0]


VIEW = ("xl", "z")
FRAME = ("y", "xh")
SWAP = [(0, 1), (1, 0)]


def across(value):
    pairs = []
    for xl in range(2):
        for xh in range(2):
            for core in range(2):
                target = (1 - xl) * 4 + (xh ^ core) * 2 + core
                pairs.append((xl * 4 + xh * 2 + core, target))
    return lax.ppermute(value, ("xl", "xh", "c"), pairs)


def along(value, steps):
    return lax.ppermute(value, "z", [(i, (i + steps) % 8) for i in range(8)])


def opposite(ahead, behind):
    value = jnp.where(lax.axis_index("c") == 0, ahead, behind)
    pairs = []
    for z in range(8):
        pairs += [(2 * z, (z + 1) % 8 * 2), (2 * z + 1, (z - 1) % 8 * 2 + 1)]
    return lax.ppermute(value, ("z", "c"), pairs)


def per_device(tokens, w_cross_qkv, w_cross_out, w_temporal_qkv, w_temporal_out):
    own = tokens[0]
    rows, features = own.shape
    half = features // 2
    core_index = lax.axis_index("c")
    core = core_index.astype(jnp.int32).reshape(1)
    place = jnp.stack([core_index, lax.axis_index("xl"), lax.axis_index("z")]).astype(jnp.int32)
    views = lax.axis_size(VIEW)
    forward = [(i, (i + 1) % views) for i in range(views)]
    backward = [(i, (i - 1) % views) for i in range(views)]

    swap = lambda value: lax.ppermute(value, "c", SWAP)
    partner = swap(own)
    before, after = (lax.ppermute(own, VIEW, pairs) for pairs in (forward, backward))

    sides = [
        jnp.concatenate(
            [
                w[:, start + side * half : start + (side + 1) * half]
                for w, start in (
                    (w_temporal_qkv, 0),
                    (w_temporal_qkv, features),
                    (w_temporal_qkv, 2 * features),
                    (w_temporal_out, 0),
                )
            ],
            axis=1,
        )
        for side in range(2)
    ]
    shard = jnp.where(core_index == 0, sides[0], sides[1])
    w_query, w_key, w_value = (
        lax.dynamic_slice_in_dim(w_cross_qkv, which * features + core_index * half, half, 1)
        for which in range(3)
    )
    weights = (w_key, w_value)
    queries, *projected = cross_project((own, partner), (*weights, w_query))
    shard, queries = lax.optimization_barrier((shard, queries))
    blocks = [jnp.concatenate([shard, across(shard)], axis=0)]
    blocks += [along(blocks[0], 1), along(blocks[0], -1)]
    state = list(cross_attend(queries, projected))
    before, after, state[0] = lax.optimization_barrier((before, after, state[0]))
    arrived = (before, after, swap(before), swap(after))
    projected = cross_project(arrived, weights)
    theirs = cross_attend(queries, projected, state, part=1)
    blocks[1], blocks[2], theirs = lax.optimization_barrier((blocks[1], blocks[2], theirs))
    blocks += [along(blocks[1], 1), along(blocks[2], -1)]
    other = swap(theirs)
    mine = cross_attend(queries, projected, state, part=0)
    *blocks, other, mine = lax.optimization_barrier((*blocks, other, mine))
    cross_rows, normed = cross_out(core, mine, other, own, w_cross_out)

    blocks += [along(blocks[3], 1), along(blocks[4], -1)]
    blocks += [opposite(blocks[5], blocks[6])]
    frames = lax.axis_size(FRAME)
    spread = lax.all_to_all(normed, FRAME, split_axis=0, concat_axis=0, tiled=True)
    *blocks, spread = lax.optimization_barrier((*blocks, spread))
    gathered = assemble(place, blocks)
    spread = spread.reshape(frames, rows // frames, features)
    gathered_other = swap(gathered)
    attended = temporal_mine(place, spread, gathered)
    gathered_other, attended = lax.optimization_barrier((gathered_other, attended))
    updated = temporal_other(place, spread, gathered, gathered_other, attended)
    temporal_rows = lax.all_to_all(
        updated.reshape(rows, features), FRAME, split_axis=0, concat_axis=0, tiled=True
    )
    return (cross_rows[None], temporal_rows[None])


def solution(mesh):
    fine = Mesh(mesh.devices.reshape(2, 8, 4, 2, 2), ("xl", "z", "y", "xh", "c"))
    by_token = P(VIEW, FRAME + ("c",), None)
    placed = (by_token, P(), P(), P(VIEW, None), P(VIEW, None))
    return jax.shard_map(
        per_device,
        mesh=fine,
        in_specs=placed,
        out_specs=(by_token, by_token),
        check_vma=False,
    )
```

profile of v0, /device:TPU:1, one launch (start us, length us, event | category | flops | bytes accessed | tf_op | source)
XLA Modules:
  0.0 118.0 jit_solution(4794023891428751883)
XLA Ops:
  0.6 3.3 %collective-permute-start = (bf16[384,1024]{1,0:T(8,128)(2,1)}, bf16[384,1024]{1,0:T(8,128)(2,1)S(1)}, u32[]{:S(2)}, u32[]{:S(2)}) collective-permute-start(bf16[384,1024]{1,0:T(8,128)(2,1)} %bitcast.9), channel_id=1, source_target_pairs={{0,1},{1,0},{2,3},{3,2},{4,5},{5,4},{6,7},{7,6},{8,9},{9,8},{10,11... | collective-permute-start | bytes 2359304 | tf_op jit(solution)/shard_map/ppermute | solution.py:343
  4.0 4.8 %collective-permute-start.5 = (bf16[384,1024]{1,0:T(8,128)(2,1)}, bf16[384,1024]{1,0:T(8,128)(2,1)S(1)}, u32[]{:S(2)}, u32[]{:S(2)}) collective-permute-start(bf16[384,1024]{1,0:T(8,128)(2,1)} %bitcast.11), channel_id=1, source_target_pairs={{0,240},{16,0},{32,16},{48,32},{64,48},{80,64},{96,80},{112,96},{1... | collective-permute-start | bytes 2359304 | tf_op jit(solution)/shard_map/ppermute | solution.py:345
  8.7 2.1 %constant_dynamic-slice_fusion = (bf16[1024,512]{1,0:T(8,128)(2,1)S(1)}, bf16[1024,512]{1,0:T(8,128)(2,1)S(1)}, bf16[1024,512]{1,0:T(8,128)(2,1)S(1)}) fusion(bf16[1024,3072]{1,0:T(8,128)(2,1)} %param.6, s32[]{:T(128)S(6)} %select_n.29, s32[]{:T(128)S(6)} %select_n.27, s32[]{:T(128)S(6)} %select_n.28), kind=kLoop, calls=%fused_computation.4 | loop fusion | bytes 6291468 | tf_op jit(solution)/shard_map/dynamic_slice | solution.py:364
  12.0 3.4 %cross_project.1 = (bf16[4,768,128]{2,1,0:T(8,128)(2,1)S(1)}, bf16[4,128,768]{2,1,0:T(8,128)(2,1)S(1)}, bf16[4,768,256]{2,1,0:T(8,128)(2,1)S(1)}) custom-call(bf16[384,1024]{1,0:T(8,128)(2,1)S(1)} %bitcast.12, bf16[384,1024]{1,0:T(8,128)(2,1)S(1)} %collective-permute-done.x1_ref, bf16[1024,512]{1,0:T(8,128)(2,1)S(1)} %get-tuple-element.75.wk_ref.refs_4_, ...), custom_call_target="tpu_custom_call" | custom-call | flops 1000000 | bytes 100000 | tf_op jit(solution)/shard_map/cross_project/pallas_call | solution.py:121
  15.4 1.9 %collective-permute-start.1 = (bf16[64,2048]{1,0:T(8,128)(2,1)S(1)}, bf16[64,2048]{1,0:T(8,128)(2,1)S(1)}, u32[]{:S(2)}, u32[]{:S(2)}) collective-permute-start(bf16[64,2048]{1,0:T(8,128)(2,1)S(1)} %maximum_select_fusion), channel_id=1, source_target_pairs={{0,128},{1,131},{2,130},{3,129},{128,0},{129,3},{130,2},{131,1},{4... | collective-permute-start | bytes 786440 | tf_op jit(solution)/shard_map/ppermute | solution.py:317
  17.3 6.5 %cross_attend.1 = (f32[4,768,128]{2,1,0:T(8,128)S(1)}, f32[4,768,128]{2,1,0:T(8,128)S(1)}, f32[4,768,128]{2,1,0:T(8,128)S(1)}) custom-call(bf16[4,768,128]{2,1,0:T(8,128)(2,1)S(1)} %get-tuple-element.40.q_ref, bf16[4,128,768]{2,1,0:T(8,128)(2,1)S(1)} %get-tuple-element.41.kt_ref, bf16[4,768,256]{2,1,0:T(8,128)(2,1)S(1)} %get-tuple-element.42.v_ref), custom_call_target="tpu_custom_call" | custom-call | flops 1000000 | bytes 100000 | tf_op jit(solution)/shard_map/cross_attend/pallas_call | solution.py:121
  23.8 3.0 %collective-permute-done.4.refs_0_ = bf16[384,1024]{1,0:T(8,128)(2,1)S(1)} collective-permute-done((bf16[384,1024]{1,0:T(8,128)(2,1)}, bf16[384,1024]{1,0:T(8,128)(2,1)S(1)}, u32[]{:S(2)}, u32[]{:S(2)}) %collective-permute-start.4) | collective-permute-done | bytes 786464 | tf_op jit(solution)/shard_map/ppermute | solution.py:345
  27.7 2.9 %collective-permute-start.3 = (bf16[128,2048]{1,0:T(8,128)(2,1)S(1)}, bf16[128,2048]{1,0:T(8,128)(2,1)S(1)}, u32[]{:S(2)}, u32[]{:S(2)}) collective-permute-start(bf16[128,2048]{1,0:T(8,128)(2,1)S(1)} %constant_dynamic-update-slice_fusion.refs_0_), channel_id=1, source_target_pairs={{0,112},{16,0},{32,16},{48,32},{64,48},{80,64},{96,80},{112,96},{1... | collective-permute-start | bytes 1572872 | tf_op jit(solution)/shard_map/ppermute | solution.py:321
  30.6 5.0 %cross_project_more.1 = (bf16[4,128,1536]{2,1,0:T(8,128)(2,1)S(1)}, bf16[4,1536,256]{2,1,0:T(8,128)(2,1)S(1)}) custom-call(bf16[384,1024]{1,0:T(8,128)(2,1)S(1)} %collective-permute-done.4.refs_0_, bf16[384,1024]{1,0:T(8,128)(2,1)S(1)} %collective-permute-done.5.refs_1_, bf16[384,1024]{1,0:T(8,128)(2,1)S(1)} %collective-permute-done.6.refs_2_, ...), custom_call_target="tpu_custom_call" | custom-call | flops 1000000 | bytes 100000 | tf_op jit(solution)/shard_map/cross_project_more/pallas_call | solution.py:121
  35.6 7.1 %cross_finish.2 = bf16[4,384,128]{2,1,0:T(8,128)(2,1)S(1)} custom-call(bf16[4,768,128]{2,1,0:T(8,128)(2,1)S(1)} %get-tuple-element.40.q_ref, bf16[4,128,1536]{2,1,0:T(8,128)(2,1)S(1)} %get-tuple-element.46.kt_ref, bf16[4,1536,256]{2,1,0:T(8,128)(2,1)S(1)} %get-tuple-element.47.v_ref, f32[4,768,128]{2,1,0:T(8,128)S(1)} %get-tuple-element.48.o_ref, ...), custom_call_target="tpu_custom_call" | custom-call | flops 1000000 | bytes 100000 | tf_op jit(solution)/shard_map/cross_finish/pallas_call | solution.py:121
  43.0 2.4 %collective-permute-start.9 = (bf16[128,2048]{1,0:T(8,128)(2,1)S(1)}, bf16[128,2048]{1,0:T(8,128)(2,1)}, u32[]{:S(2)}, u32[]{:S(2)}) collective-permute-start(bf16[128,2048]{1,0:T(8,128)(2,1)S(1)} %collective-permute-done.3.refs_2_), channel_id=1, source_target_pairs={{0,112},{16,0},{32,16},{48,32},{64,48},{80,64},{96,80},{112,96},{1... | collective-permute-start | bytes 1572872 | tf_op jit(solution)/shard_map/ppermute | solution.py:321
  45.5 3.5 %collective-permute-start.10 = (bf16[4,384,128]{2,1,0:T(8,128)(2,1)S(1)}, bf16[4,384,128]{2,1,0:T(8,128)(2,1)S(1)}, u32[]{:S(2)}, u32[]{:S(2)}) collective-permute-start(bf16[4,384,128]{2,1,0:T(8,128)(2,1)S(1)} %cross_finish.2), channel_id=1, source_target_pairs={{0,1},{1,0},{2,3},{3,2},{4,5},{5,4},{6,7},{7,6},{8,9},{9,8},{10,11... | collective-permute-start | bytes 1179656 | tf_op jit(solution)/shard_map/ppermute | solution.py:343
  49.0 7.1 %cross_finish.3.mine_ref = bf16[4,384,128]{2,1,0:T(8,128)(2,1)S(1)} custom-call(bf16[4,768,128]{2,1,0:T(8,128)(2,1)S(1)} %get-tuple-element.40.q_ref, bf16[4,128,1536]{2,1,0:T(8,128)(2,1)S(1)} %get-tuple-element.46.kt_ref, bf16[4,1536,256]{2,1,0:T(8,128)(2,1)S(1)} %get-tuple-element.47.v_ref, f32[4,768,128]{2,1,0:T(8,128)S(1)} %get-tuple-element.48.o_ref, ...), custom_call_target="tpu_custom_call" | custom-call | flops 1000000 | bytes 100000 | tf_op jit(solution)/shard_map/cross_finish/pallas_call | solution.py:121
  56.1 1.5 %collective-permute-start.11 = (bf16[128,2048]{1,0:T(8,128)(2,1)}, bf16[128,2048]{1,0:T(8,128)(2,1)S(1)}, u32[]{:S(2)}, u32[]{:S(2)}) collective-permute-start(bf16[128,2048]{1,0:T(8,128)(2,1)} %collective-permute-done.8.refs_3_), channel_id=1, source_target_pairs={{0,16},{16,32},{32,48},{48,64},{64,80},{80,96},{96,112},{112,0},{1... | collective-permute-start | bytes 1572872 | tf_op jit(solution)/shard_map/ppermute | solution.py:321
  58.8 2.2 %cross_out.1 = (bf16[384,1024]{1,0:T(8,128)(2,1)}, bf16[384,1024]{1,0:T(8,128)(2,1)}) custom-call(s32[1]{0:T(128)} %bitcast.core_ref, bf16[4,384,128]{2,1,0:T(8,128)(2,1)S(1)} %cross_finish.3.mine_ref, bf16[4,384,128]{2,1,0:T(8,128)(2,1)S(1)} %collective-permute-done.10.other_ref, bf16[384,1024]{1,0:T(8,128)(2,1)S(1)} %bitcast.13, ...), custom_call_target="tpu_custom_call" | custom-call | flops 1000000 | bytes 100000 | tf_op jit(solution)/shard_map/cross_out/pallas_call | solution.py:121
  61.1 6.6 %all-to-all-start = ((bf16[8,48,1024]{2,1,0:T(8,128)(2,1)}), bf16[8,48,1024]{2,1,0:T(8,128)(2,1)S(1)}, u32[]{:S(2)}, u32[]{:S(2)}) async-start(bf16[8,48,1024]{2,1,0:T(8,128)(2,1)} %bitcast.5), calls=%async_computation | async-start | bytes 1572864 | tf_op jit(solution)/shard_map/all_to_all | solution.py:387
  69.9 2.1 %collective-permute-start.13 = (bf16[128,2048]{1,0:T(8,128)(2,1)}, bf16[128,2048]{1,0:T(8,128)(2,1)}, u32[]{:S(2)}, u32[]{:S(2)}) collective-permute-start(bf16[128,2048]{1,0:T(8,128)(2,1)} %broadcast_select_fusion), channel_id=1, source_target_pairs={{0,16},{1,113},{16,32},{17,1},{32,48},{33,17},{48,64},{49,33},{64,... | collective-permute-start | bytes 1572872 | tf_op jit(solution)/shard_map/ppermute | solution.py:329
  72.1 6.6 %all-to-all-done = bf16[8,48,1024]{2,1,0:T(8,128)(2,1)S(1)} async-done(((bf16[8,48,1024]{2,1,0:T(8,128)(2,1)}), bf16[8,48,1024]{2,1,0:T(8,128)(2,1)S(1)}, u32[]{:S(2)}, u32[]{:S(2)}) %all-to-all-start) | async-done | bytes 786464 | tf_op jit(solution)/shard_map/all_to_all | solution.py:387
  78.7 1.6 %assemble.1.w_ref.wm_ref = bf16[1024,2048]{1,0:T(8,128)(2,1)S(1)} custom-call(s32[3]{0:T(128)S(1)} %pad_add_fusion.place_ref, bf16[128,2048]{1,0:T(8,128)(2,1)S(1)} %constant_dynamic-update-slice_fusion.refs_0_, bf16[128,2048]{1,0:T(8,128)(2,1)S(1)} %collective-permute-done.2.refs_1_, bf16[128,2048]{1,0:T(8,128)(2,1)S(1)} %collective-permute-done.3.refs_2_, ...), custom_call_target="tpu_custom_call" | custom-call | flops 1000000 | bytes 100000 | tf_op jit(solution)/shard_map/assemble/pallas_call | solution.py:121
  80.3 5.4 %collective-permute-start.14 = (bf16[1024,2048]{1,0:T(8,128)(2,1)S(1)}, bf16[1024,2048]{1,0:T(8,128)(2,1)S(1)}, u32[]{:S(2)}, u32[]{:S(2)}) collective-permute-start(bf16[1024,2048]{1,0:T(8,128)(2,1)S(1)} %assemble.1.w_ref.wm_ref), channel_id=1, source_target_pairs={{0,1},{1,0},{2,3},{3,2},{4,5},{5,4},{6,7},{7,6},{8,9},{9,8},{10,11... | collective-permute-start | bytes 12582920 | tf_op jit(solution)/shard_map/ppermute | solution.py:343
  85.7 3.6 %temporal_mine.1.att_ref = bf16[384,512]{1,0:T(8,128)(2,1)S(1)} custom-call(s32[3]{0:T(128)S(1)} %pad_add_fusion.place_ref, bf16[8,48,1024]{2,1,0:T(8,128)(2,1)S(1)} %all-to-all-done, bf16[1024,2048]{1,0:T(8,128)(2,1)S(1)} %assemble.1.w_ref.wm_ref), custom_call_target="tpu_custom_call" | custom-call | flops 1000000 | bytes 100000 | tf_op jit(solution)/shard_map/temporal_mine/pallas_call | solution.py:121
  89.3 3.2 %collective-permute-done.14.wo_ref = bf16[1024,2048]{1,0:T(8,128)(2,1)S(1)} collective-permute-done((bf16[1024,2048]{1,0:T(8,128)(2,1)S(1)}, bf16[1024,2048]{1,0:T(8,128)(2,1)S(1)}, u32[]{:S(2)}, u32[]{:S(2)}) %collective-permute-start.14) | collective-permute-done | bytes 4194336 | tf_op jit(solution)/shard_map/ppermute | solution.py:343
  92.5 4.6 %temporal_other.1 = bf16[8,48,1024]{2,1,0:T(8,128)(2,1)S(1)} custom-call(s32[3]{0:T(128)S(1)} %pad_add_fusion.place_ref, bf16[8,48,1024]{2,1,0:T(8,128)(2,1)S(1)} %all-to-all-done, bf16[1024,2048]{1,0:T(8,128)(2,1)S(1)} %assemble.1.w_ref.wm_ref, bf16[1024,2048]{1,0:T(8,128)(2,1)S(1)} %collective-permute-done.14.wo_ref, bf16[384,512]{1,0:T(8,128)(2,1)S(1)} %temporal_mine.1.att_ref), custom_call_target="tpu_custom_call" | custom-call | flops 1000000 | bytes 100000 | tf_op jit(solution)/shard_map/temporal_other/pallas_call | solution.py:121
  97.1 20.0 %all_to_all.18 = bf16[8,48,1024]{2,1,0:T(8,128)(2,1)S(1)} all-to-all(bf16[8,48,1024]{2,1,0:T(8,128)(2,1)S(1)} %temporal_other.1), channel_id=1, replica_groups=mesh['xl'=2,'z'=8,'y'=4,'xh'=2,'c'=2] {'y','xh'}, dimensions={0} | all-to-all | bytes 1572864 | tf_op jit(solution)/shard_map/all_to_all | solution.py:395
  (34 shorter events, 6.7 us)
Async XLA Ops:
  0.6 10.4 %collective-permute-start = (bf16[384,1024]{1,0:T(8,128)(2,1)}, bf16[384,1024]{1,0:T(8,128)(2,1)S(1)}, u32[]{:S(2)}, u32[]{:S(2)}) collective-permute-start(bf16[384,1024]{1,0:T(8,128)(2,1)} %bitcast.9), channel_id=1, source_target_pairs={{0,1},{1,0},{2,3},{3,2},{4,5},{5,4},{6,7},{7,6},{8,9},{9,8},{10,11... | collective-permute-start | bytes 2359304 | tf_op jit(solution)/shard_map/ppermute | solution.py:343
  4.0 22.8 %collective-permute-start.4 = (bf16[384,1024]{1,0:T(8,128)(2,1)}, bf16[384,1024]{1,0:T(8,128)(2,1)S(1)}, u32[]{:S(2)}, u32[]{:S(2)}) collective-permute-start(bf16[384,1024]{1,0:T(8,128)(2,1)} %bitcast.10), channel_id=1, source_target_pairs={{0,16},{16,32},{32,48},{48,64},{64,80},{80,96},{96,112},{112,128},... | collective-permute-start | bytes 2359304 | tf_op jit(solution)/shard_map/ppermute | solution.py:345
  4.0 22.8 %collective-permute-start.5 = (bf16[384,1024]{1,0:T(8,128)(2,1)}, bf16[384,1024]{1,0:T(8,128)(2,1)S(1)}, u32[]{:S(2)}, u32[]{:S(2)}) collective-permute-start(bf16[384,1024]{1,0:T(8,128)(2,1)} %bitcast.11), channel_id=1, source_target_pairs={{0,240},{16,0},{32,16},{48,32},{64,48},{80,64},{96,80},{112,96},{1... | collective-permute-start | bytes 2359304 | tf_op jit(solution)/shard_map/ppermute | solution.py:345
  8.7 2.1 %copy-start.2 = (bf16[64,3072]{1,0:T(8,128)(2,1)S(1)}, bf16[64,3072]{1,0:T(8,128)(2,1)}, u32[]{:S(2)}) copy-start(bf16[64,3072]{1,0:T(8,128)(2,1)} %param.8) | copy-start | bytes 1179652
  8.7 2.2 %copy-start.3 = (bf16[64,1024]{1,0:T(8,128)(2,1)S(1)}, bf16[64,1024]{1,0:T(8,128)(2,1)}, u32[]{:S(2)}) copy-start(bf16[64,1024]{1,0:T(8,128)(2,1)} %param.9) | copy-start | bytes 393220
  10.9 1.1 copy-start
  15.4 12.1 %collective-permute-start.1 = (bf16[64,2048]{1,0:T(8,128)(2,1)S(1)}, bf16[64,2048]{1,0:T(8,128)(2,1)S(1)}, u32[]{:S(2)}, u32[]{:S(2)}) collective-permute-start(bf16[64,2048]{1,0:T(8,128)(2,1)S(1)} %maximum_select_fusion), channel_id=1, source_target_pairs={{0,128},{1,131},{2,130},{3,129},{128,0},{129,3},{130,2},{131,1},{4... | collective-permute-start | bytes 786440 | tf_op jit(solution)/shard_map/ppermute | solution.py:317
  26.8 3.8 %collective-permute-start.6 = (bf16[384,1024]{1,0:T(8,128)(2,1)S(1)}, bf16[384,1024]{1,0:T(8,128)(2,1)S(1)}, u32[]{:S(2)}, u32[]{:S(2)}) collective-permute-start(bf16[384,1024]{1,0:T(8,128)(2,1)S(1)} %collective-permute-done.4.refs_0_), channel_id=1, source_target_pairs={{0,1},{1,0},{2,3},{3,2},{4,5},{5,4},{6,7},{7,6},{8,9},{9,8},{10,11... | collective-permute-start | bytes 2359304 | tf_op jit(solution)/shard_map/ppermute | solution.py:343
  27.5 3.1 %collective-permute-start.7 = (bf16[384,1024]{1,0:T(8,128)(2,1)S(1)}, bf16[384,1024]{1,0:T(8,128)(2,1)S(1)}, u32[]{:S(2)}, u32[]{:S(2)}) collective-permute-start(bf16[384,1024]{1,0:T(8,128)(2,1)S(1)} %collective-permute-done.5.refs_1_), channel_id=1, source_target_pairs={{0,1},{1,0},{2,3},{3,2},{4,5},{5,4},{6,7},{7,6},{8,9},{9,8},{10,11... | collective-permute-start | bytes 2359304 | tf_op jit(solution)/shard_map/ppermute | solution.py:343
  27.6 15.1 %collective-permute-start.2 = (bf16[128,2048]{1,0:T(8,128)(2,1)S(1)}, bf16[128,2048]{1,0:T(8,128)(2,1)S(1)}, u32[]{:S(2)}, u32[]{:S(2)}) collective-permute-start(bf16[128,2048]{1,0:T(8,128)(2,1)S(1)} %constant_dynamic-update-slice_fusion.refs_0_), channel_id=1, source_target_pairs={{0,16},{16,32},{32,48},{48,64},{64,80},{80,96},{96,112},{112,0},{1... | collective-permute-start | bytes 1572872 | tf_op jit(solution)/shard_map/ppermute | solution.py:321
  27.7 15.0 %collective-permute-start.3 = (bf16[128,2048]{1,0:T(8,128)(2,1)S(1)}, bf16[128,2048]{1,0:T(8,128)(2,1)S(1)}, u32[]{:S(2)}, u32[]{:S(2)}) collective-permute-start(bf16[128,2048]{1,0:T(8,128)(2,1)S(1)} %constant_dynamic-update-slice_fusion.refs_0_), channel_id=1, source_target_pairs={{0,112},{16,0},{32,16},{48,32},{64,48},{80,64},{96,80},{112,96},{1... | collective-permute-start | bytes 1572872 | tf_op jit(solution)/shard_map/ppermute | solution.py:321
  42.7 16.2 %copy-start.1 = (bf16[1024,1024]{1,0:T(8,128)(2,1)S(1)}, bf16[1024,1024]{1,0:T(8,128)(2,1)}, u32[]{:S(2)}) copy-start(bf16[1024,1024]{1,0:T(8,128)(2,1)} %w_ref.1) | copy-start | bytes 6291460
  42.7 13.4 %collective-permute-start.8 = (bf16[128,2048]{1,0:T(8,128)(2,1)S(1)}, bf16[128,2048]{1,0:T(8,128)(2,1)}, u32[]{:S(2)}, u32[]{:S(2)}) collective-permute-start(bf16[128,2048]{1,0:T(8,128)(2,1)S(1)} %collective-permute-done.2.refs_1_), channel_id=1, source_target_pairs={{0,16},{16,32},{32,48},{48,64},{64,80},{80,96},{96,112},{112,0},{1... | collective-permute-start | bytes 1572872 | tf_op jit(solution)/shard_map/ppermute | solution.py:321
  43.0 13.0 %collective-permute-start.9 = (bf16[128,2048]{1,0:T(8,128)(2,1)S(1)}, bf16[128,2048]{1,0:T(8,128)(2,1)}, u32[]{:S(2)}, u32[]{:S(2)}) collective-permute-start(bf16[128,2048]{1,0:T(8,128)(2,1)S(1)} %collective-permute-done.3.refs_2_), channel_id=1, source_target_pairs={{0,112},{16,0},{32,16},{48,32},{64,48},{80,64},{96,80},{112,96},{1... | collective-permute-start | bytes 1572872 | tf_op jit(solution)/shard_map/ppermute | solution.py:321
  45.5 10.6 %collective-permute-start.10 = (bf16[4,384,128]{2,1,0:T(8,128)(2,1)S(1)}, bf16[4,384,128]{2,1,0:T(8,128)(2,1)S(1)}, u32[]{:S(2)}, u32[]{:S(2)}) collective-permute-start(bf16[4,384,128]{2,1,0:T(8,128)(2,1)S(1)} %cross_finish.2), channel_id=1, source_target_pairs={{0,1},{1,0},{2,3},{3,2},{4,5},{5,4},{6,7},{7,6},{8,9},{9,8},{10,11... | collective-permute-start | bytes 1179656 | tf_op jit(solution)/shard_map/ppermute | solution.py:343
  56.1 12.7 %collective-permute-start.11 = (bf16[128,2048]{1,0:T(8,128)(2,1)}, bf16[128,2048]{1,0:T(8,128)(2,1)S(1)}, u32[]{:S(2)}, u32[]{:S(2)}) collective-permute-start(bf16[128,2048]{1,0:T(8,128)(2,1)} %collective-permute-done.8.refs_3_), channel_id=1, source_target_pairs={{0,16},{16,32},{32,48},{48,64},{64,80},{80,96},{96,112},{112,0},{1... | collective-permute-start | bytes 1572872 | tf_op jit(solution)/shard_map/ppermute | solution.py:321
  57.6 11.4 %collective-permute-start.12 = (bf16[128,2048]{1,0:T(8,128)(2,1)}, bf16[128,2048]{1,0:T(8,128)(2,1)S(1)}, u32[]{:S(2)}, u32[]{:S(2)}) collective-permute-start(bf16[128,2048]{1,0:T(8,128)(2,1)} %collective-permute-done.9.refs_4_), channel_id=1, source_target_pairs={{0,112},{16,0},{32,16},{48,32},{64,48},{80,64},{96,80},{112,96},{1... | collective-permute-start | bytes 1572872 | tf_op jit(solution)/shard_map/ppermute | solution.py:321
  61.1 17.6 %all-to-all-start = ((bf16[8,48,1024]{2,1,0:T(8,128)(2,1)}), bf16[8,48,1024]{2,1,0:T(8,128)(2,1)S(1)}, u32[]{:S(2)}, u32[]{:S(2)}) async-start(bf16[8,48,1024]{2,1,0:T(8,128)(2,1)} %bitcast.5), calls=%async_computation | async-start | bytes 1572864 | tf_op jit(solution)/shard_map/all_to_all | solution.py:387
  69.9 8.8 %collective-permute-start.13 = (bf16[128,2048]{1,0:T(8,128)(2,1)}, bf16[128,2048]{1,0:T(8,128)(2,1)}, u32[]{:S(2)}, u32[]{:S(2)}) collective-permute-start(bf16[128,2048]{1,0:T(8,128)(2,1)} %broadcast_select_fusion), channel_id=1, source_target_pairs={{0,16},{1,113},{16,32},{17,1},{32,48},{33,17},{48,64},{49,33},{64,... | collective-permute-start | bytes 1572872 | tf_op jit(solution)/shard_map/ppermute | solution.py:329
  80.3 12.2 %collective-permute-start.14 = (bf16[1024,2048]{1,0:T(8,128)(2,1)S(1)}, bf16[1024,2048]{1,0:T(8,128)(2,1)S(1)}, u32[]{:S(2)}, u32[]{:S(2)}) collective-permute-start(bf16[1024,2048]{1,0:T(8,128)(2,1)S(1)} %assemble.1.w_ref.wm_ref), channel_id=1, source_target_pairs={{0,1},{1,0},{2,3},{3,2},{4,5},{5,4},{6,7},{7,6},{8,9},{9,8},{10,11... | collective-permute-start | bytes 12582920 | tf_op jit(solution)/shard_map/ppermute | solution.py:343
where the time goes:
time: 118 us
  Pallas kernels  41 us (35%)
  starting transfers between devices  36.9 us (31%)
  blocking collectives  20 us (17%)
  waiting for transfers between devices  14.2 us (12%)
  local copies, waits for them, and re-layouts  4.1 us (3%)
    pallas_call x9, Pallas kernels, local_kernel(): pl.pallas_call(kernel, in_specs=[SMEM_SPEC] * scalars + [VMEM_SPEC] * (le...  41 us
    all_to_all x1, blocking collectives, per_device(): lax.all_to_all(updated.reshape(rows, features), FRAME, split_axis=0, conc...  20 us
    ppermute x5, starting transfers between devices, per_device(): swap = lambda value: lax.ppermute(value, 'c', SWAP)  13 us
    ppermute x6, starting transfers between devices, along(): return lax.ppermute(value, 'z', [(i, (i + steps) % 8) for i in range(8)])  8.52 us
    all_to_all x1, starting transfers between devices, per_device(): lax.all_to_all(normed, FRAME, split_axis=0, concat_axis=0, tiled=True)  6.61 us
    all_to_all x1, waiting for transfers between devices, per_device(): lax.all_to_all(normed, FRAME, split_axis=0, concat_axis=0, tiled=True)  6.61 us
    ppermute x2, starting transfers between devices, per_device(): lax.ppermute(own, VIEW, pairs)  4.77 us
    ppermute x5, waiting for transfers between devices, per_device(): swap = lambda value: lax.ppermute(value, 'c', SWAP)  3.24 us
  transfers between devices with their start and end apart: 16, of which 5 were waited for; matrix products, arithmetic and copies ran while one was open for 3% of the time, Pallas kernels for 29%

commit v1 on v0

--- a/solution.py
+++ b/solution.py
@@ -93,7 +93,7 @@
                     out[pair, rows, :] = value
         return carry
 
-    lax.fori_loop(0, pairs, attend, 0, unroll=UNROLL)
+    lax.fori_loop(0, pairs, attend, 0, unroll=1 if state is None else UNROLL)
 
 
 def project_kernel(x0_ref, x1_ref, wk_ref, wv_ref, wq_ref, q_ref, kt_ref, v_ref, norm_s):
@@ -241,65 +241,60 @@
             store(part, quad * QUAD, attended.astype(BF16))
 
 
-def temporal_mine_kernel(place_ref, x_ref, w_ref, att_ref, x_s):
+def temporal_attend_kernel(place_ref, x_ref, w_ref, att_ref, x_s):
     def store(rows, start, value):
         att_ref[rows, start : start + QUAD] = value
 
     temporal_heads(x_ref, w_ref, place_ref[1], x_s, store)
 
 
-def temporal_other_kernel(place_ref, x_ref, wm_ref, wo_ref, att_ref, out_ref, x_s, att_s):
-    features = x_ref.shape[2]
-    half = features // 2
+def temporal_out_kernel(place_ref, am_ref, ao_ref, wm_ref, wo_ref, out_ref, att_s):
+    half = am_ref.shape[1]
     core, own_half = place_ref[0], place_ref[1]
     mine, other = pl.multiple_of(core * half, half), pl.multiple_of((1 - core) * half, half)
-    att_s[:, pl.ds(mine, half)] = att_ref[...]
-
-    def store(rows, start, value):
-        att_s[rows, pl.ds(pl.multiple_of(other + start, QUAD), QUAD)] = value
-
-    temporal_heads(x_ref, wo_ref, own_half, x_s, store)
+    att_s[:, pl.ds(mine, half)] = am_ref[...]
+    att_s[:, pl.ds(other, half)] = ao_ref[...]
     for start, w_ref in ((mine, wm_ref), (other, wo_ref)):
-        made = times(att_s, w_ref, slice(3 * half, 4 * half), own_half).astype(BF16)
-        for rows, frame, place in grouped(x_ref.shape):
+        made = times(att_s, w_ref, slice(0, half), own_half).astype(BF16)
+        for rows, frame, place in grouped(out_ref.shape):
             out_ref[frame, place, pl.ds(start, half)] = made[rows]
 
 
 def assemble_kernel(place_ref, *refs):
-    blocks, out_ref = refs[:-1], refs[-1]
+    blocks, (qkv_ref, out_ref) = refs[:-2], refs[-2:]
     size = blocks[0].shape[0]
     count = out_ref.shape[0] // size
-    own = place_ref[2]
-
-    def rows(step, start, length):
-        index = lax.rem(own + step + count, count)
-        return pl.ds(pl.multiple_of(index * size + start, length), length)
-
+    cut = qkv_ref.shape[1]
     for ref, step in zip(blocks, (0, -1, 1, -2, 2, -3, 3, 4)):
-        out_ref[rows(step, 0, size), :] = ref[...]
+        index = lax.rem(place_ref[2] + step + count, count)
+        rows = pl.ds(pl.multiple_of(index * size, size), size)
+        qkv_ref[rows, :] = ref[:, :cut]
+        out_ref[rows, :] = ref[:, cut:]
 
 
 def assemble(place, blocks):
     size, columns = blocks[0].shape
-    out_shape = [jax.ShapeDtypeStruct((8 * size, columns), BF16)]
-    return local_kernel(assemble_kernel, "assemble", (place, *blocks), out_shape, (), 1)[0]
-
-
-def temporal_mine(place, rows, weights):
+    rows, cut = 8 * size, columns // 4 * 3
+    out_shape = [jax.ShapeDtypeStruct((rows, width), BF16) for width in (cut, columns - cut)]
+    return local_kernel(assemble_kernel, "assemble", (place, *blocks), out_shape, (), 1)
+
+
+def temporal_attend(place, rows, weights):
     frames, positions, features = rows.shape
     count = frames * positions
     out_shape = [jax.ShapeDtypeStruct((count, features // 2), BF16)]
     scratch = [pltpu.VMEM((count, features), BF16)]
     operands = (place, rows, weights)
-    return local_kernel(temporal_mine_kernel, "temporal_mine", operands, out_shape, scratch, 1)[0]
-
-
-def temporal_other(place, rows, mine, other, attended):
-    frames, positions, features = rows.shape
-    out_shape = [jax.ShapeDtypeStruct(rows.shape, BF16)]
-    scratch = [pltpu.VMEM((frames * positions, features), BF16)] * 2
-    operands = (place, rows, mine, other, attended)
-    return local_kernel(temporal_other_kernel, "temporal_other", operands, out_shape, scratch, 1)[0]
+    return local_kernel(
+        temporal_attend_kernel, "temporal_attend", operands, out_shape, scratch, 1
+    )[0]
+
+
+def temporal_out(place, shape, mine, other, w_mine, w_other):
+    out_shape = [jax.ShapeDtypeStruct(shape, BF16)]
+    scratch = [pltpu.VMEM((mine.shape[0], shape[2]), BF16)]
+    operands = (place, mine, other, w_mine, w_other)
+    return local_kernel(temporal_out_kernel, "temporal_out", operands, out_shape, scratch, 1)[0]
 
 
 VIEW = ("xl", "z")
@@ -386,12 +381,16 @@
     frames = lax.axis_size(FRAME)
     spread = lax.all_to_all(normed, FRAME, split_axis=0, concat_axis=0, tiled=True)
     *blocks, spread = lax.optimization_barrier((*blocks, spread))
-    gathered = assemble(place, blocks)
+    gathered, out_gathered = assemble(place, blocks)
     spread = spread.reshape(frames, rows // frames, features)
-    gathered_other = swap(gathered)
-    attended = temporal_mine(place, spread, gathered)
+    gathered_other, out_other = swap(gathered), swap(out_gathered)
+    attended = temporal_attend(place, spread, gathered)
     gathered_other, attended = lax.optimization_barrier((gathered_other, attended))
-    updated = temporal_other(place, spread, gathered, gathered_other, attended)
+    attended_other = temporal_attend(place, spread, gathered_other)
+    out_other, attended_other = lax.optimization_barrier((out_other, attended_other))
+    updated = temporal_out(
+        place, spread.shape, attended, attended_other, out_gathered, out_other
+    )
     temporal_rows = lax.all_to_all(
         updated.reshape(rows, features), FRAME, split_axis=0, concat_axis=0, tiled=True
     )

time: 118 us -> 117 us (level)
  waiting for transfers between devices: 14.2 us -> 11.1 us
  Pallas kernels: 41 us -> 42.8 us
    ppermute x5 -> x6, waiting for transfers between devices: 3.24 us -> 1.39 us  [per_device(): swap = lambda value: lax.ppermute(value, 'c', SWAP)]
    pallas_call x9 -> x10, Pallas kernels: 41 us -> 42.8 us  [local_kernel(): pl.pallas_call(kernel, in_specs=[SMEM_SPEC] * scalars + [VMEM_SPEC] * (le...]
    ppermute x2, waiting for transfers between devices: 2.99 us -> 1.7 us  [per_device(): lax.ppermute(own, VIEW, pairs)]
    ppermute x5 -> x6, starting transfers between devices: 13 us -> 13.1 us  [per_device(): swap = lambda value: lax.ppermute(value, 'c', SWAP)]
  transfers between devices with their start and end apart: 16 -> 17, of which waited for: 5 -> 5; matrix products, arithmetic and copies ran while one was open for 3% -> 3% of each run, Pallas kernels for 29% -> 34%
where the time goes in v1:
time: 117 us
  Pallas kernels  42.8 us (37%)
  starting transfers between devices  37 us (32%)
  blocking collectives  20 us (17%)
  waiting for transfers between devices  11.1 us (9%)
  local copies, waits for them, and re-layouts  4.1 us (4%)
    pallas_call x10, Pallas kernels, local_kernel(): pl.pallas_call(kernel, in_specs=[SMEM_SPEC] * scalars + [VMEM_SPEC] * (le...  42.8 us
    all_to_all x1, blocking collectives, per_device(): lax.all_to_all(updated.reshape(rows, features), FRAME, split_axis=0, conc...  20 us
    ppermute x6, starting transfers between devices, per_device(): swap = lambda value: lax.ppermute(value, 'c', SWAP)  13.1 us
    ppermute x6, starting transfers between devices, along(): return lax.ppermute(value, 'z', [(i, (i + steps) % 8) for i in range(8)])  8.52 us
    all_to_all x1, waiting for transfers between devices, per_device(): lax.all_to_all(normed, FRAME, split_axis=0, concat_axis=0, tiled=True)  6.62 us
    all_to_all x1, starting transfers between devices, per_device(): lax.all_to_all(normed, FRAME, split_axis=0, concat_axis=0, tiled=True)  6.61 us
    ppermute x2, starting transfers between devices, per_device(): lax.ppermute(own, VIEW, pairs)  4.77 us
  transfers between devices with their start and end apart: 17, of which 5 were waited for; matrix products, arithmetic and copies ran while one was open for 3% of the time, Pallas kernels for 34%

profile of v1, /device:TPU:1, one launch (start us, length us, event | category | flops | bytes accessed | tf_op | source)
XLA Modules:
  0.0 116.8 jit_solution(4286412417342135990)
XLA Ops:
  0.6 3.3 %collective-permute-start = (bf16[384,1024]{1,0:T(8,128)(2,1)}, bf16[384,1024]{1,0:T(8,128)(2,1)S(1)}, u32[]{:S(2)}, u32[]{:S(2)}) collective-permute-start(bf16[384,1024]{1,0:T(8,128)(2,1)} %bitcast.9), channel_id=1, source_target_pairs={{0,1},{1,0},{2,3},{3,2},{4,5},{5,4},{6,7},{7,6},{8,9},{9,8},{10,11... | collective-permute-start | bytes 2359304 | tf_op jit(solution)/shard_map/ppermute | solution.py:338
  4.0 4.8 %collective-permute-start.5 = (bf16[384,1024]{1,0:T(8,128)(2,1)}, bf16[384,1024]{1,0:T(8,128)(2,1)S(1)}, u32[]{:S(2)}, u32[]{:S(2)}) collective-permute-start(bf16[384,1024]{1,0:T(8,128)(2,1)} %bitcast.11), channel_id=1, source_target_pairs={{0,240},{16,0},{32,16},{48,32},{64,48},{80,64},{96,80},{112,96},{1... | collective-permute-start | bytes 2359304 | tf_op jit(solution)/shard_map/ppermute | solution.py:340
  8.7 2.1 %constant_dynamic-slice_fusion = (bf16[1024,512]{1,0:T(8,128)(2,1)S(1)}, bf16[1024,512]{1,0:T(8,128)(2,1)S(1)}, bf16[1024,512]{1,0:T(8,128)(2,1)S(1)}) fusion(bf16[1024,3072]{1,0:T(8,128)(2,1)} %param.6, s32[]{:T(128)S(6)} %select_n.29, s32[]{:T(128)S(6)} %select_n.27, s32[]{:T(128)S(6)} %select_n.28), kind=kLoop, calls=%fused_computation.4 | loop fusion | bytes 6291468 | tf_op jit(solution)/shard_map/dynamic_slice | solution.py:359
  12.0 3.4 %cross_project.1 = (bf16[4,768,128]{2,1,0:T(8,128)(2,1)S(1)}, bf16[4,128,768]{2,1,0:T(8,128)(2,1)S(1)}, bf16[4,768,256]{2,1,0:T(8,128)(2,1)S(1)}) custom-call(bf16[384,1024]{1,0:T(8,128)(2,1)S(1)} %bitcast.12, bf16[384,1024]{1,0:T(8,128)(2,1)S(1)} %collective-permute-done.x1_ref, bf16[1024,512]{1,0:T(8,128)(2,1)S(1)} %get-tuple-element.83.wk_ref.refs_4_, ...), custom_call_target="tpu_custom_call" | custom-call | flops 1000000 | bytes 100000 | tf_op jit(solution)/shard_map/cross_project/pallas_call | solution.py:121
  15.4 1.9 %collective-permute-start.1 = (bf16[64,2048]{1,0:T(8,128)(2,1)S(1)}, bf16[64,2048]{1,0:T(8,128)(2,1)S(1)}, u32[]{:S(2)}, u32[]{:S(2)}) collective-permute-start(bf16[64,2048]{1,0:T(8,128)(2,1)S(1)} %maximum_select_fusion), channel_id=1, source_target_pairs={{0,128},{1,131},{2,130},{3,129},{128,0},{129,3},{130,2},{131,1},{4... | collective-permute-start | bytes 786440 | tf_op jit(solution)/shard_map/ppermute | solution.py:312
  17.3 7.7 %cross_attend.1 = (f32[4,768,128]{2,1,0:T(8,128)S(1)}, f32[4,768,128]{2,1,0:T(8,128)S(1)}, f32[4,768,128]{2,1,0:T(8,128)S(1)}) custom-call(bf16[4,768,128]{2,1,0:T(8,128)(2,1)S(1)} %get-tuple-element.44.q_ref, bf16[4,128,768]{2,1,0:T(8,128)(2,1)S(1)} %get-tuple-element.45.kt_ref, bf16[4,768,256]{2,1,0:T(8,128)(2,1)S(1)} %get-tuple-element.46.v_ref), custom_call_target="tpu_custom_call" | custom-call | flops 1000000 | bytes 100000 | tf_op jit(solution)/shard_map/cross_attend/pallas_call | solution.py:121
  25.1 1.7 %collective-permute-done.4.refs_0_ = bf16[384,1024]{1,0:T(8,128)(2,1)S(1)} collective-permute-done((bf16[384,1024]{1,0:T(8,128)(2,1)}, bf16[384,1024]{1,0:T(8,128)(2,1)S(1)}, u32[]{:S(2)}, u32[]{:S(2)}) %collective-permute-start.4) | collective-permute-done | bytes 786464 | tf_op jit(solution)/shard_map/ppermute | solution.py:340
  27.7 2.9 %collective-permute-start.3 = (bf16[128,2048]{1,0:T(8,128)(2,1)S(1)}, bf16[128,2048]{1,0:T(8,128)(2,1)S(1)}, u32[]{:S(2)}, u32[]{:S(2)}) collective-permute-start(bf16[128,2048]{1,0:T(8,128)(2,1)S(1)} %constant_dynamic-update-slice_fusion.refs_0_), channel_id=1, source_target_pairs={{0,112},{16,0},{32,16},{48,32},{64,48},{80,64},{96,80},{112,96},{1... | collective-permute-start | bytes 1572872 | tf_op jit(solution)/shard_map/ppermute | solution.py:316
  30.6 5.0 %cross_project_more.1 = (bf16[4,128,1536]{2,1,0:T(8,128)(2,1)S(1)}, bf16[4,1536,256]{2,1,0:T(8,128)(2,1)S(1)}) custom-call(bf16[384,1024]{1,0:T(8,128)(2,1)S(1)} %collective-permute-done.4.refs_0_, bf16[384,1024]{1,0:T(8,128)(2,1)S(1)} %collective-permute-done.5.refs_1_, bf16[384,1024]{1,0:T(8,128)(2,1)S(1)} %collective-permute-done.6.refs_2_, ...), custom_call_target="tpu_custom_call" | custom-call | flops 1000000 | bytes 100000 | tf_op jit(solution)/shard_map/cross_project_more/pallas_call | solution.py:121
  35.6 7.1 %cross_finish.2 = bf16[4,384,128]{2,1,0:T(8,128)(2,1)S(1)} custom-call(bf16[4,768,128]{2,1,0:T(8,128)(2,1)S(1)} %get-tuple-element.44.q_ref, bf16[4,128,1536]{2,1,0:T(8,128)(2,1)S(1)} %get-tuple-element.50.kt_ref, bf16[4,1536,256]{2,1,0:T(8,128)(2,1)S(1)} %get-tuple-element.51.v_ref, f32[4,768,128]{2,1,0:T(8,128)S(1)} %get-tuple-element.52.o_ref, ...), custom_call_target="tpu_custom_call" | custom-call | flops 1000000 | bytes 100000 | tf_op jit(solution)/shard_map/cross_finish/pallas_call | solution.py:121
  43.0 2.4 %collective-permute-start.9 = (bf16[128,2048]{1,0:T(8,128)(2,1)S(1)}, bf16[128,2048]{1,0:T(8,128)(2,1)}, u32[]{:S(2)}, u32[]{:S(2)}) collective-permute-start(bf16[128,2048]{1,0:T(8,128)(2,1)S(1)} %collective-permute-done.3.refs_2_), channel_id=1, source_target_pairs={{0,112},{16,0},{32,16},{48,32},{64,48},{80,64},{96,80},{112,96},{1... | collective-permute-start | bytes 1572872 | tf_op jit(solution)/shard_map/ppermute | solution.py:316
  45.5 3.5 %collective-permute-start.10 = (bf16[4,384,128]{2,1,0:T(8,128)(2,1)S(1)}, bf16[4,384,128]{2,1,0:T(8,128)(2,1)S(1)}, u32[]{:S(2)}, u32[]{:S(2)}) collective-permute-start(bf16[4,384,128]{2,1,0:T(8,128)(2,1)S(1)} %cross_finish.2), channel_id=1, source_target_pairs={{0,1},{1,0},{2,3},{3,2},{4,5},{5,4},{6,7},{7,6},{8,9},{9,8},{10,11... | collective-permute-start | bytes 1179656 | tf_op jit(solution)/shard_map/ppermute | solution.py:338
  49.0 7.1 %cross_finish.3.mine_ref = bf16[4,384,128]{2,1,0:T(8,128)(2,1)S(1)} custom-call(bf16[4,768,128]{2,1,0:T(8,128)(2,1)S(1)} %get-tuple-element.44.q_ref, bf16[4,128,1536]{2,1,0:T(8,128)(2,1)S(1)} %get-tuple-element.50.kt_ref, bf16[4,1536,256]{2,1,0:T(8,128)(2,1)S(1)} %get-tuple-element.51.v_ref, f32[4,768,128]{2,1,0:T(8,128)S(1)} %get-tuple-element.52.o_ref, ...), custom_call_target="tpu_custom_call" | custom-call | flops 1000000 | bytes 100000 | tf_op jit(solution)/shard_map/cross_finish/pallas_call | solution.py:121
  56.1 1.5 %collective-permute-start.11 = (bf16[128,2048]{1,0:T(8,128)(2,1)}, bf16[128,2048]{1,0:T(8,128)(2,1)S(1)}, u32[]{:S(2)}, u32[]{:S(2)}) collective-permute-start(bf16[128,2048]{1,0:T(8,128)(2,1)} %collective-permute-done.8.refs_3_), channel_id=1, source_target_pairs={{0,16},{16,32},{32,48},{48,64},{64,80},{80,96},{96,112},{112,0},{1... | collective-permute-start | bytes 1572872 | tf_op jit(solution)/shard_map/ppermute | solution.py:316
  58.8 2.2 %cross_out.1 = (bf16[384,1024]{1,0:T(8,128)(2,1)}, bf16[384,1024]{1,0:T(8,128)(2,1)}) custom-call(s32[1]{0:T(128)} %bitcast.core_ref, bf16[4,384,128]{2,1,0:T(8,128)(2,1)S(1)} %cross_finish.3.mine_ref, bf16[4,384,128]{2,1,0:T(8,128)(2,1)S(1)} %collective-permute-done.10.other_ref, bf16[384,1024]{1,0:T(8,128)(2,1)S(1)} %bitcast.13, ...), custom_call_target="tpu_custom_call" | custom-call | flops 1000000 | bytes 100000 | tf_op jit(solution)/shard_map/cross_out/pallas_call | solution.py:121
  61.1 6.6 %all-to-all-start = ((bf16[8,48,1024]{2,1,0:T(8,128)(2,1)}), bf16[8,48,1024]{2,1,0:T(8,128)(2,1)S(1)}, u32[]{:S(2)}, u32[]{:S(2)}) async-start(bf16[8,48,1024]{2,1,0:T(8,128)(2,1)} %bitcast.5), calls=%async_computation | async-start | bytes 1572864 | tf_op jit(solution)/shard_map/all_to_all | solution.py:382
  69.9 2.1 %collective-permute-start.13 = (bf16[128,2048]{1,0:T(8,128)(2,1)}, bf16[128,2048]{1,0:T(8,128)(2,1)}, u32[]{:S(2)}, u32[]{:S(2)}) collective-permute-start(bf16[128,2048]{1,0:T(8,128)(2,1)} %broadcast_select_fusion), channel_id=1, source_target_pairs={{0,16},{1,113},{16,32},{17,1},{32,48},{33,17},{48,64},{49,33},{64,... | collective-permute-start | bytes 1572872 | tf_op jit(solution)/shard_map/ppermute | solution.py:324
  72.1 6.6 %all-to-all-done = bf16[8,48,1024]{2,1,0:T(8,128)(2,1)S(1)} async-done(((bf16[8,48,1024]{2,1,0:T(8,128)(2,1)}), bf16[8,48,1024]{2,1,0:T(8,128)(2,1)S(1)}, u32[]{:S(2)}, u32[]{:S(2)}) %all-to-all-start) | async-done | bytes 786464 | tf_op jit(solution)/shard_map/all_to_all | solution.py:382
  78.7 1.6 %assemble.1 = (bf16[1024,1536]{1,0:T(8,128)(2,1)S(1)}, bf16[1024,512]{1,0:T(8,128)(2,1)S(1)}) custom-call(s32[3]{0:T(128)S(1)} %pad_add_fusion.place_ref, bf16[128,2048]{1,0:T(8,128)(2,1)S(1)} %constant_dynamic-update-slice_fusion.refs_0_, bf16[128,2048]{1,0:T(8,128)(2,1)S(1)} %collective-permute-done.2.refs_1_, ...), custom_call_target="tpu_custom_call" | custom-call | flops 1000000 | bytes 100000 | tf_op jit(solution)/shard_map/assemble/pallas_call | solution.py:121
  80.3 5.1 %collective-permute-start.14 = (bf16[1024,1536]{1,0:T(8,128)(2,1)S(1)}, bf16[1024,1536]{1,0:T(8,128)(2,1)S(1)}, u32[]{:S(2)}, u32[]{:S(2)}) collective-permute-start(bf16[1024,1536]{1,0:T(8,128)(2,1)S(1)} %get-tuple-element.75.w_ref), channel_id=1, source_target_pairs={{0,1},{1,0},{2,3},{3,2},{4,5},{5,4},{6,7},{7,6},{8,9},{9,8},{10,11... | collective-permute-start | bytes 9437192 | tf_op jit(solution)/shard_map/ppermute | solution.py:338
  85.8 3.5 %temporal_attend.2.am_ref = bf16[384,512]{1,0:T(8,128)(2,1)S(1)} custom-call(s32[3]{0:T(128)S(1)} %pad_add_fusion.place_ref, bf16[8,48,1024]{2,1,0:T(8,128)(2,1)S(1)} %all-to-all-done, bf16[1024,1536]{1,0:T(8,128)(2,1)S(1)} %get-tuple-element.75.w_ref), custom_call_target="tpu_custom_call" | custom-call | flops 1000000 | bytes 100000 | tf_op jit(solution)/shard_map/temporal_attend/pallas_call | solution.py:121
  90.8 3.5 %temporal_attend.3.ao_ref = bf16[384,512]{1,0:T(8,128)(2,1)S(1)} custom-call(s32[3]{0:T(128)S(1)} %pad_add_fusion.place_ref, bf16[8,48,1024]{2,1,0:T(8,128)(2,1)S(1)} %all-to-all-done, bf16[1024,1536]{1,0:T(8,128)(2,1)S(1)} %collective-permute-done.14.w_ref), custom_call_target="tpu_custom_call" | custom-call | flops 1000000 | bytes 100000 | tf_op jit(solution)/shard_map/temporal_attend/pallas_call | solution.py:121
  94.3 1.6 %temporal_out.1 = bf16[8,48,1024]{2,1,0:T(8,128)(2,1)S(1)} custom-call(s32[3]{0:T(128)S(1)} %pad_add_fusion.place_ref, bf16[384,512]{1,0:T(8,128)(2,1)S(1)} %temporal_attend.2.am_ref, bf16[384,512]{1,0:T(8,128)(2,1)S(1)} %temporal_attend.3.ao_ref, bf16[1024,512]{1,0:T(8,128)(2,1)S(1)} %get-tuple-element.78.wm_ref, ...), custom_call_target="tpu_custom_call" | custom-call | flops 1000000 | bytes 100000 | tf_op jit(solution)/shard_map/temporal_out/pallas_call | solution.py:121
  95.9 20.0 %all_to_all.18 = bf16[8,48,1024]{2,1,0:T(8,128)(2,1)S(1)} all-to-all(bf16[8,48,1024]{2,1,0:T(8,128)(2,1)S(1)} %temporal_out.1), channel_id=1, replica_groups=mesh['xl'=2,'z'=8,'y'=4,'xh'=2,'c'=2] {'y','xh'}, dimensions={0} | all-to-all | bytes 1572864 | tf_op jit(solution)/shard_map/all_to_all | solution.py:394
  (37 shorter events, 8.5 us)
Async XLA Ops:
  0.6 10.4 %collective-permute-start = (bf16[384,1024]{1,0:T(8,128)(2,1)}, bf16[384,1024]{1,0:T(8,128)(2,1)S(1)}, u32[]{:S(2)}, u32[]{:S(2)}) collective-permute-start(bf16[384,1024]{1,0:T(8,128)(2,1)} %bitcast.9), channel_id=1, source_target_pairs={{0,1},{1,0},{2,3},{3,2},{4,5},{5,4},{6,7},{7,6},{8,9},{9,8},{10,11... | collective-permute-start | bytes 2359304 | tf_op jit(solution)/shard_map/ppermute | solution.py:338
  4.0 22.8 %collective-permute-start.4 = (bf16[384,1024]{1,0:T(8,128)(2,1)}, bf16[384,1024]{1,0:T(8,128)(2,1)S(1)}, u32[]{:S(2)}, u32[]{:S(2)}) collective-permute-start(bf16[384,1024]{1,0:T(8,128)(2,1)} %bitcast.10), channel_id=1, source_target_pairs={{0,16},{16,32},{32,48},{48,64},{64,80},{80,96},{96,112},{112,128},... | collective-permute-start | bytes 2359304 | tf_op jit(solution)/shard_map/ppermute | solution.py:340
  4.0 22.8 %collective-permute-start.5 = (bf16[384,1024]{1,0:T(8,128)(2,1)}, bf16[384,1024]{1,0:T(8,128)(2,1)S(1)}, u32[]{:S(2)}, u32[]{:S(2)}) collective-permute-start(bf16[384,1024]{1,0:T(8,128)(2,1)} %bitcast.11), channel_id=1, source_target_pairs={{0,240},{16,0},{32,16},{48,32},{64,48},{80,64},{96,80},{112,96},{1... | collective-permute-start | bytes 2359304 | tf_op jit(solution)/shard_map/ppermute | solution.py:340
  8.7 2.1 %copy-start.2 = (bf16[64,3072]{1,0:T(8,128)(2,1)S(1)}, bf16[64,3072]{1,0:T(8,128)(2,1)}, u32[]{:S(2)}) copy-start(bf16[64,3072]{1,0:T(8,128)(2,1)} %param.8) | copy-start | bytes 1179652
  8.7 2.2 %copy-start.3 = (bf16[64,1024]{1,0:T(8,128)(2,1)S(1)}, bf16[64,1024]{1,0:T(8,128)(2,1)}, u32[]{:S(2)}) copy-start(bf16[64,1024]{1,0:T(8,128)(2,1)} %param.9) | copy-start | bytes 393220
  10.9 1.1 copy-start
  15.4 12.1 %collective-permute-start.1 = (bf16[64,2048]{1,0:T(8,128)(2,1)S(1)}, bf16[64,2048]{1,0:T(8,128)(2,1)S(1)}, u32[]{:S(2)}, u32[]{:S(2)}) collective-permute-start(bf16[64,2048]{1,0:T(8,128)(2,1)S(1)} %maximum_select_fusion), channel_id=1, source_target_pairs={{0,128},{1,131},{2,130},{3,129},{128,0},{129,3},{130,2},{131,1},{4... | collective-permute-start | bytes 786440 | tf_op jit(solution)/shard_map/ppermute | solution.py:312
  26.8 3.8 %collective-permute-start.6 = (bf16[384,1024]{1,0:T(8,128)(2,1)S(1)}, bf16[384,1024]{1,0:T(8,128)(2,1)S(1)}, u32[]{:S(2)}, u32[]{:S(2)}) collective-permute-start(bf16[384,1024]{1,0:T(8,128)(2,1)S(1)} %collective-permute-done.4.refs_0_), channel_id=1, source_target_pairs={{0,1},{1,0},{2,3},{3,2},{4,5},{5,4},{6,7},{7,6},{8,9},{9,8},{10,11... | collective-permute-start | bytes 2359304 | tf_op jit(solution)/shard_map/ppermute | solution.py:338
  27.5 3.1 %collective-permute-start.7 = (bf16[384,1024]{1,0:T(8,128)(2,1)S(1)}, bf16[384,1024]{1,0:T(8,128)(2,1)S(1)}, u32[]{:S(2)}, u32[]{:S(2)}) collective-permute-start(bf16[384,1024]{1,0:T(8,128)(2,1)S(1)} %collective-permute-done.5.refs_1_), channel_id=1, source_target_pairs={{0,1},{1,0},{2,3},{3,2},{4,5},{5,4},{6,7},{7,6},{8,9},{9,8},{10,11... | collective-permute-start | bytes 2359304 | tf_op jit(solution)/shard_map/ppermute | solution.py:338
  27.6 15.1 %collective-permute-start.2 = (bf16[128,2048]{1,0:T(8,128)(2,1)S(1)}, bf16[128,2048]{1,0:T(8,128)(2,1)S(1)}, u32[]{:S(2)}, u32[]{:S(2)}) collective-permute-start(bf16[128,2048]{1,0:T(8,128)(2,1)S(1)} %constant_dynamic-update-slice_fusion.refs_0_), channel_id=1, source_target_pairs={{0,16},{16,32},{32,48},{48,64},{64,80},{80,96},{96,112},{112,0},{1... | collective-permute-start | bytes 1572872 | tf_op jit(solution)/shard_map/ppermute | solution.py:316
  27.7 15.0 %collective-permute-start.3 = (bf16[128,2048]{1,0:T(8,128)(2,1)S(1)}, bf16[128,2048]{1,0:T(8,128)(2,1)S(1)}, u32[]{:S(2)}, u32[]{:S(2)}) collective-permute-start(bf16[128,2048]{1,0:T(8,128)(2,1)S(1)} %constant_dynamic-update-slice_fusion.refs_0_), channel_id=1, source_target_pairs={{0,112},{16,0},{32,16},{48,32},{64,48},{80,64},{96,80},{112,96},{1... | collective-permute-start | bytes 1572872 | tf_op jit(solution)/shard_map/ppermute | solution.py:316
  42.7 16.2 %copy-start.1 = (bf16[1024,1024]{1,0:T(8,128)(2,1)S(1)}, bf16[1024,1024]{1,0:T(8,128)(2,1)}, u32[]{:S(2)}) copy-start(bf16[1024,1024]{1,0:T(8,128)(2,1)} %w_ref.1) | copy-start | bytes 6291460
  42.7 13.4 %collective-permute-start.8 = (bf16[128,2048]{1,0:T(8,128)(2,1)S(1)}, bf16[128,2048]{1,0:T(8,128)(2,1)}, u32[]{:S(2)}, u32[]{:S(2)}) collective-permute-start(bf16[128,2048]{1,0:T(8,128)(2,1)S(1)} %collective-permute-done.2.refs_1_), channel_id=1, source_target_pairs={{0,16},{16,32},{32,48},{48,64},{64,80},{80,96},{96,112},{112,0},{1... | collective-permute-start | bytes 1572872 | tf_op jit(solution)/shard_map/ppermute | solution.py:316
  43.0 13.0 %collective-permute-start.9 = (bf16[128,2048]{1,0:T(8,128)(2,1)S(1)}, bf16[128,2048]{1,0:T(8,128)(2,1)}, u32[]{:S(2)}, u32[]{:S(2)}) collective-permute-start(bf16[128,2048]{1,0:T(8,128)(2,1)S(1)} %collective-permute-done.3.refs_2_), channel_id=1, source_target_pairs={{0,112},{16,0},{32,16},{48,32},{64,48},{80,64},{96,80},{112,96},{1... | collective-permute-start | bytes 1572872 | tf_op jit(solution)/shard_map/ppermute | solution.py:316
  45.5 10.6 %collective-permute-start.10 = (bf16[4,384,128]{2,1,0:T(8,128)(2,1)S(1)}, bf16[4,384,128]{2,1,0:T(8,128)(2,1)S(1)}, u32[]{:S(2)}, u32[]{:S(2)}) collective-permute-start(bf16[4,384,128]{2,1,0:T(8,128)(2,1)S(1)} %cross_finish.2), channel_id=1, source_target_pairs={{0,1},{1,0},{2,3},{3,2},{4,5},{5,4},{6,7},{7,6},{8,9},{9,8},{10,11... | collective-permute-start | bytes 1179656 | tf_op jit(solution)/shard_map/ppermute | solution.py:338
  56.1 12.7 %collective-permute-start.11 = (bf16[128,2048]{1,0:T(8,128)(2,1)}, bf16[128,2048]{1,0:T(8,128)(2,1)S(1)}, u32[]{:S(2)}, u32[]{:S(2)}) collective-permute-start(bf16[128,2048]{1,0:T(8,128)(2,1)} %collective-permute-done.8.refs_3_), channel_id=1, source_target_pairs={{0,16},{16,32},{32,48},{48,64},{64,80},{80,96},{96,112},{112,0},{1... | collective-permute-start | bytes 1572872 | tf_op jit(solution)/shard_map/ppermute | solution.py:316
  57.6 11.4 %collective-permute-start.12 = (bf16[128,2048]{1,0:T(8,128)(2,1)}, bf16[128,2048]{1,0:T(8,128)(2,1)S(1)}, u32[]{:S(2)}, u32[]{:S(2)}) collective-permute-start(bf16[128,2048]{1,0:T(8,128)(2,1)} %collective-permute-done.9.refs_4_), channel_id=1, source_target_pairs={{0,112},{16,0},{32,16},{48,32},{64,48},{80,64},{96,80},{112,96},{1... | collective-permute-start | bytes 1572872 | tf_op jit(solution)/shard_map/ppermute | solution.py:316
  61.1 17.6 %all-to-all-start = ((bf16[8,48,1024]{2,1,0:T(8,128)(2,1)}), bf16[8,48,1024]{2,1,0:T(8,128)(2,1)S(1)}, u32[]{:S(2)}, u32[]{:S(2)}) async-start(bf16[8,48,1024]{2,1,0:T(8,128)(2,1)} %bitcast.5), calls=%async_computation | async-start | bytes 1572864 | tf_op jit(solution)/shard_map/all_to_all | solution.py:382
  69.9 8.8 %collective-permute-start.13 = (bf16[128,2048]{1,0:T(8,128)(2,1)}, bf16[128,2048]{1,0:T(8,128)(2,1)}, u32[]{:S(2)}, u32[]{:S(2)}) collective-permute-start(bf16[128,2048]{1,0:T(8,128)(2,1)} %broadcast_select_fusion), channel_id=1, source_target_pairs={{0,16},{1,113},{16,32},{17,1},{32,48},{33,17},{48,64},{49,33},{64,... | collective-permute-start | bytes 1572872 | tf_op jit(solution)/shard_map/ppermute | solution.py:324
  80.3 10.4 %collective-permute-start.14 = (bf16[1024,1536]{1,0:T(8,128)(2,1)S(1)}, bf16[1024,1536]{1,0:T(8,128)(2,1)S(1)}, u32[]{:S(2)}, u32[]{:S(2)}) collective-permute-start(bf16[1024,1536]{1,0:T(8,128)(2,1)S(1)} %get-tuple-element.75.w_ref), channel_id=1, source_target_pairs={{0,1},{1,0},{2,3},{3,2},{4,5},{5,4},{6,7},{7,6},{8,9},{9,8},{10,11... | collective-permute-start | bytes 9437192 | tf_op jit(solution)/shard_map/ppermute | solution.py:338
  85.5 8.8 %collective-permute-start.15 = (bf16[1024,512]{1,0:T(8,128)(2,1)S(1)}, bf16[1024,512]{1,0:T(8,128)(2,1)S(1)}, u32[]{:S(2)}, u32[]{:S(2)}) collective-permute-start(bf16[1024,512]{1,0:T(8,128)(2,1)S(1)} %get-tuple-element.78.wm_ref), channel_id=1, source_target_pairs={{0,1},{1,0},{2,3},{3,2},{4,5},{5,4},{6,7},{7,6},{8,9},{9,8},{10,11... | collective-permute-start | bytes 3145736 | tf_op jit(solution)/shard_map/ppermute | solution.py:338
